TPU v7x, 1024 devices: a whole 4x8x16 slice. The times are simulated.
1024 devices in a mesh: domain: 64 (over x_hi, z, core), band: 16 (over y, x_lo).
Axes of the slice: x: 4 (x_hi: 2, x_lo: 2; x = x_hi * 2 + x_lo), y: 8, z: 16, core: 2. Of those that a mesh axis runs over, the one named last changes fastest.
Arguments:
- orbitals: float32 [64, 1024, 16, 128], P('band', 'domain'), may hold values from -50 to 50
- potential: float32 [1024, 16, 128], P('domain'), may hold values from -3 to 1
- projectors: float32 [2048, 32768], P('domain'), may hold values from -0.5 to 0.5
- slot_ids: int32 [2048], P('domain'), may hold values from 0 to 1023, as said below
- slot_count: int32 [64], P('domain'), may hold values from 16 to 32, as said below
- energies: float32 [1024], replicated, may hold values from 1 to 4
Outputs:
- filtered: float32 [64, 1024, 16, 128], P('band', 'domain')
- margin: float32 [64, 64], P('band')
Inputs may be any that keep to these rules, and one draw needn't show every extreme that they name: `slot_ids`: device d owns projectors d * 16 to (d + 1) * 16 - 1. The first 16 slots of block d name its own projectors, each once; its other slots name projectors owned by blocks that share a face with it, and a projector may be named by several slots. Slots 0 to slot_count[d] - 1 of block d are live, the rest are padding; some block has all 32 slots live.
All inputs are finite; a program needn't handle non-finite values.
Results may differ from a plain program's by a relative error of at most 0.00035.
Values may be sent and summed in bfloat16 or wider, within the bound.
A program may use at most 64 MiB of HBM per device.

v0:
```python
import jax
import jax.numpy as jnp
from jax import lax
from jax.sharding import PartitionSpec as P

STENCIL = (
    -5369.0 / 1800.0,
    12.0 / 7.0,
    -15.0 / 56.0,
    10.0 / 189.0,
    -1.0 / 112.0,
    2.0 / 1925.0,
    -1.0 / 16632.0,
)
SPACING = 0.5
CENTER = 27.5
HALF_WIDTH = 22.5


def from_partner(value, axis, distance):
    mask = 2**distance
    pairs = [(source, source ^ mask) for source in range(lax.axis_size(axis))]
    return lax.ppermute(value, axis, pairs)


def contract_cells(left_side, right_side):
    return lax.dot_general(
        left_side,
        right_side,
        (((1,), (1,)), ((), ())),
        precision=lax.Precision.HIGHEST,
        preferred_element_type=jnp.float32,
    )


def on_device(orbitals, potential, projectors, slot_ids, slot_count, energies):
    orbital_rows = orbitals.shape[0]
    cell_count = orbitals.shape[1] * orbitals.shape[2] * orbitals.shape[3]
    domains = lax.axis_size("domain")
    blocks_z = min(4, domains)
    blocks_y = min(4, domains // blocks_z)
    device_index = lax.axis_index("domain")
    digits = (
        device_index // (blocks_y * blocks_z),
        device_index // blocks_z % blocks_y,
        device_index % blocks_z,
    )
    bits_z = blocks_z.bit_length() - 1
    bits_y = blocks_y.bit_length() - 1
    low_bits = (bits_z + bits_y, bits_z, 0)
    radius = len(STENCIL) - 1
    slot_total = projectors.shape[0]
    proj_total = energies.shape[0]
    highest = lax.Precision.HIGHEST
    active_slots = (jnp.arange(slot_total, dtype=jnp.int32) < slot_count[0]).astype(jnp.float32)
    selector = (slot_ids[:, None] == jnp.arange(proj_total, dtype=jnp.int32)[None, :]).astype(
        jnp.float32
    )

    def extend(values, dimension):
        length = values.shape[dimension]
        lower_face = lax.slice_in_dim(values, 0, radius, axis=dimension)
        upper_face = lax.slice_in_dim(values, length - radius, length, axis=dimension)
        first_bit = low_bits[dimension - 1]
        second_bit = first_bit + 1
        digit = digits[dimension - 1]
        leading = jnp.logical_or(digit == 0, digit == 3)
        send_first = jnp.where(leading, upper_face, lower_face)
        got_first = from_partner(send_first.astype(jnp.bfloat16), "domain", first_bit).astype(
            send_first.dtype
        )
        send_second = jnp.where(leading, lower_face, upper_face)
        got_second = from_partner(send_second.astype(jnp.bfloat16), "domain", second_bit).astype(
            send_second.dtype
        )
        above = jnp.where(leading, got_first, got_second)
        below = jnp.where(leading, got_second, got_first)
        return jnp.concatenate([below, values, above], axis=dimension)

    def kinetic(values):
        summed = 3.0 * STENCIL[0] * values
        for dimension in (1, 2, 3):
            padded = extend(values, dimension)
            length = values.shape[dimension]
            for offset in range(1, radius + 1):
                above = lax.slice_in_dim(
                    padded, radius + offset, radius + offset + length, axis=dimension
                )
                below = lax.slice_in_dim(
                    padded, radius - offset, radius - offset + length, axis=dimension
                )
                summed = summed + STENCIL[offset] * (below + above)
        return -0.5 / (SPACING * SPACING) * summed

    def project(values):
        flattened = values.reshape(orbital_rows, cell_count)
        partial_value = contract_cells(flattened, projectors) * active_slots[None, :]
        local_coef = jnp.dot(partial_value, selector, precision=highest)
        coefficient = lax.psum(local_coef, "domain")
        weights = (
            jnp.dot(coefficient * energies[None, :], selector.T, precision=highest)
            * active_slots[None, :]
        )
        term = jnp.dot(weights, projectors, precision=highest)
        return term.reshape(values.shape)

    def hamiltonian(values):
        return kinetic(values) + potential[None] * values + project(values)

    first = (hamiltonian(orbitals) - CENTER * orbitals) / HALF_WIDTH
    filtered = 2.0 * (hamiltonian(first) - CENTER * first) / HALF_WIDTH - orbitals
    rounded = filtered.astype(jnp.bfloat16).reshape(orbital_rows, cell_count)
    total_cells = cell_count * domains
    product = lax.dot_general(
        rounded,
        lax.all_gather(rounded, "band", axis=0, tiled=True),
        (((1,), (1,)), ((), ())),
        preferred_element_type=jnp.float32,
    )
    margin = lax.psum(product, "domain") / total_cells
    return (filtered, margin)


def solution(mesh):
    in_specs = (
        P("band", "domain", None, None),
        P("domain", None, None),
        P("domain", None),
        P("domain"),
        P("domain"),
        P(),
    )
    out_specs = (P("band", "domain", None, None), P("band", None))
    return jax.shard_map(
        on_device, mesh=mesh, in_specs=in_specs, out_specs=out_specs, check_vma=False
    )
```

profile of v0, /device:TPU:1, one launch (start us, length us, event | category | flops | bytes accessed | tf_op | source)
XLA Modules:
  0.0 875.0 jit_solution(17273179780897925046)
XLA Ops:
  7.3 1.1 select_convert_fusion.11
  8.3 5.5 collective-permute-start
  13.8 19.1 %collective-permute-start.1 = (bf16[4,6,16,128]{3,2,1,0:T(8,128)(2,1)S(1)}, bf16[4,6,16,128]{3,2,1,0:T(8,128)(2,1)S(1)}, u32[]{:S(2)}, u32[]{:S(2)}) collective-permute-start(bf16[4,6,16,128]{3,2,1,0:T(8,128)(2,1)S(1)} %get-tuple-element.15), channel_id=1, source_target_pairs={{0,256},{16,272},{32,288},{48,304},{64,320},{80,336},{96,352},{112... | collective-permute-start | bytes 294920 | tf_op jit(solution)/shard_map/ppermute | solution.py:23
  32.9 1.1 select_convert_fusion.7
  34.0 5.8 collective-permute-start.2
  39.9 1.4 select_convert_fusion.3
  41.2 3.1 collective-permute-start.4
  44.3 3.7 collective-permute-start.5
  48.7 5.7 convolution_multiply_fusion.3
  54.7 250.1 %psum.21 = f32[4,1024]{1,0:T(4,128)S(1)} all-reduce(f32[4,1024]{1,0:T(4,128)S(1)} %fusion.176), channel_id=1, replica_groups=mesh['domain'=64,'band'=16] {'domain'}, use_global_device_ids=true, to_apply=%region_0.1 | all-reduce | flops 4096 | bytes 32768 | tf_op jit(solution)/shard_map/psum | solution.py:99
  305.0 4.4 convolution_bitcast_fusion.1
  309.4 2.2 collective-permute-start.3
  311.8 4.5 collective-permute-done.3
  316.4 3.4 broadcast_multiply_fusion
  320.0 3.4 convolution_multiply_fusion.1
  323.4 0.2 fusion.175
  323.6 257.3 %psum.22 = f32[4,1024]{1,0:T(4,128)S(1)} all-reduce(f32[4,1024]{1,0:T(4,128)S(1)} %fusion.175), channel_id=1, replica_groups=mesh['domain'=64,'band'=16] {'domain'}, use_global_device_ids=true, to_apply=%region_1.2 | all-reduce | flops 4096 | bytes 32768 | tf_op jit(solution)/shard_map/psum | solution.py:99
  581.1 2.0 collective-permute-start.6
  583.1 1.9 collective-permute-start.7
  585.0 1.9 collective-permute-start.8
  586.9 4.2 collective-permute-start.10
  591.2 5.8 collective-permute-start.11
  596.9 4.3 convolution_bitcast_fusion
  601.2 10.6 %collective-permute-start.9 = (bf16[4,16,6,128]{3,2,1,0:T(8,128)(2,1)S(1)}, bf16[4,16,6,128]{3,2,1,0:T(8,128)(2,1)S(1)}, u32[]{:S(2)}, u32[]{:S(2)}) collective-permute-start(bf16[4,16,6,128]{3,2,1,0:T(8,128)(2,1)S(1)} %get-tuple-element.9), channel_id=1, source_target_pairs={{0,64},{16,80},{32,96},{48,112},{64,0},{80,16},{96,32},{112,48},{1... | collective-permute-start | bytes 294920 | tf_op jit(solution)/shard_map/ppermute | solution.py:23
  612.0 5.8 collective-permute-done.9
  617.9 4.1 fusion.185
  622.0 0.8 reshape.32
  622.8 102.2 %all-gather.3.cloned.1.call-done = bf16[16,4,32768]{2,1,0:T(4,128)(2,1)} async-done(((bf16[1,4,32768]{2,1,0:T(4,128)(2,1)}), bf16[16,4,32768]{2,1,0:T(4,128)(2,1)}) %all-gather.3.cloned.1.call-update) | async-done | bytes 4194320 | tf_op jit(solution)/shard_map/all_gather | solution.py:116
  725.1 7.0 reshape.33
  732.1 3.4 fusion.172
  735.4 132.1 %psum.23 = f32[4,64]{1,0:T(4,128)S(1)} all-reduce(f32[4,64]{1,0:T(4,128)S(1)} %fusion.172), channel_id=1, replica_groups=mesh['domain'=64,'band'=16] {'domain'}, use_global_device_ids=true, to_apply=%region_2.3 | all-reduce | flops 256 | bytes 2048 | tf_op jit(solution)/shard_map/psum | solution.py:120
  867.6 0.6 broadcast_multiply_fusion.2
  (38 shorter events, 1.3 us)
Async XLA Ops:
  7.2 47.3 %copy-start.4 = (s32[32]{0:T(128)S(1)}, s32[32]{0:T(128)}, u32[]{:S(2)}) copy-start(s32[32]{0:T(128)} %param.9) | copy-start | bytes 388
  7.2 297.6 %copy-start.3 = (f32[1024]{0:T(1024)S(1)}, f32[1024]{0:T(1024)}, u32[]{:S(2)}) copy-start(f32[1024]{0:T(1024)} %param.11) | copy-start | bytes 12292
  7.2 717.9 %all-gather.3.cloned.1.call-start = ((), (), s32[]{:S(2)}) async-start(), calls=%async_computation | async-start | bytes 4456448 | tf_op jit(solution)/shard_map/all_gather | solution.py:116
  8.3 303.4 %collective-permute-start = (bf16[4,6,16,128]{3,2,1,0:T(8,128)(2,1)S(1)}, bf16[4,6,16,128]{3,2,1,0:T(8,128)(2,1)S(1)}, u32[]{:S(2)}, u32[]{:S(2)}) collective-permute-start(bf16[4,6,16,128]{3,2,1,0:T(8,128)(2,1)S(1)} %get-tuple-element.14), channel_id=1, source_target_pairs={{0,512},{16,528},{32,544},{48,560},{64,576},{80,592},{96,608},{112... | collective-permute-start | bytes 294920 | tf_op jit(solution)/shard_map/ppermute | solution.py:23
  13.8 297.9 %collective-permute-start.1 = (bf16[4,6,16,128]{3,2,1,0:T(8,128)(2,1)S(1)}, bf16[4,6,16,128]{3,2,1,0:T(8,128)(2,1)S(1)}, u32[]{:S(2)}, u32[]{:S(2)}) collective-permute-start(bf16[4,6,16,128]{3,2,1,0:T(8,128)(2,1)S(1)} %get-tuple-element.15), channel_id=1, source_target_pairs={{0,256},{16,272},{32,288},{48,304},{64,320},{80,336},{96,352},{112... | collective-permute-start | bytes 294920 | tf_op jit(solution)/shard_map/ppermute | solution.py:23
  34.0 277.8 %collective-permute-start.2 = (bf16[4,16,6,128]{3,2,1,0:T(8,128)(2,1)S(1)}, bf16[4,16,6,128]{3,2,1,0:T(8,128)(2,1)S(1)}, u32[]{:S(2)}, u32[]{:S(2)}) collective-permute-start(bf16[4,16,6,128]{3,2,1,0:T(8,128)(2,1)S(1)} %get-tuple-element.16), channel_id=1, source_target_pairs={{0,128},{16,144},{32,160},{48,176},{64,192},{80,208},{96,224},{112... | collective-permute-start | bytes 294920 | tf_op jit(solution)/shard_map/ppermute | solution.py:23
  41.2 268.2 %collective-permute-start.4 = (bf16[4,16,16,6]{3,2,1,0:T(8,128)(2,1)S(1)}, bf16[4,16,16,6]{3,2,1,0:T(8,128)(2,1)S(1)}, u32[]{:S(2)}, u32[]{:S(2)}) collective-permute-start(bf16[4,16,16,6]{3,2,1,0:T(8,128)(2,1)S(1)} %get-tuple-element.20), channel_id=1, source_target_pairs={{0,32},{16,48},{32,0},{48,16},{64,96},{80,112},{96,64},{112,80},{1... | collective-permute-start | bytes 36872 | tf_op jit(solution)/shard_map/ppermute | solution.py:23
  44.3 267.3 %collective-permute-start.5 = (bf16[4,16,16,6]{3,2,1,0:T(8,128)(2,1)S(1)}, bf16[4,16,16,6]{3,2,1,0:T(8,128)(2,1)S(1)}, u32[]{:S(2)}, u32[]{:S(2)}) collective-permute-start(bf16[4,16,16,6]{3,2,1,0:T(8,128)(2,1)S(1)} %get-tuple-element.21), channel_id=1, source_target_pairs={{0,16},{16,0},{32,48},{48,32},{64,80},{80,64},{96,112},{112,96},{1... | collective-permute-start | bytes 36872 | tf_op jit(solution)/shard_map/ppermute | solution.py:23
  48.7 260.6 %copy-start.2 = (f32[16,16,128]{2,1,0:T(8,128)S(1)}, f32[16,16,128]{2,1,0:T(8,128)}, u32[]{:S(2)}) copy-start(f32[16,16,128]{2,1,0:T(8,128)} %param.7) | copy-start | bytes 393220
  305.0 11.4 %copy-start.1 = (f32[4,16,16,128]{3,2,1,0:T(8,128)S(1)}, f32[4,16,16,128]{3,2,1,0:T(8,128)}, u32[]{:S(2)}) copy-start(f32[4,16,16,128]{3,2,1,0:T(8,128)} %param.6) | copy-start | bytes 1572868
  309.4 10.6 %copy-start = (f32[32,32768]{1,0:T(8,128)S(1)}, f32[32,32768]{1,0:T(8,128)}, u32[]{:S(2)}) copy-start(f32[32,32768]{1,0:T(8,128)} %param.8) | copy-start | bytes 12582916
  309.4 6.9 collective-permute-start.3
  581.1 30.8 %collective-permute-start.6 = (bf16[4,6,16,128]{3,2,1,0:T(8,128)(2,1)S(1)}, bf16[4,6,16,128]{3,2,1,0:T(8,128)(2,1)S(1)}, u32[]{:S(2)}, u32[]{:S(2)}) collective-permute-start(bf16[4,6,16,128]{3,2,1,0:T(8,128)(2,1)S(1)} %get-tuple-element.6), channel_id=1, source_target_pairs={{0,512},{16,528},{32,544},{48,560},{64,576},{80,592},{96,608},{112... | collective-permute-start | bytes 294920 | tf_op jit(solution)/shard_map/ppermute | solution.py:23
  583.1 28.9 %collective-permute-start.7 = (bf16[4,6,16,128]{3,2,1,0:T(8,128)(2,1)S(1)}, bf16[4,6,16,128]{3,2,1,0:T(8,128)(2,1)S(1)}, u32[]{:S(2)}, u32[]{:S(2)}) collective-permute-start(bf16[4,6,16,128]{3,2,1,0:T(8,128)(2,1)S(1)} %get-tuple-element.7), channel_id=1, source_target_pairs={{0,256},{16,272},{32,288},{48,304},{64,320},{80,336},{96,352},{112... | collective-permute-start | bytes 294920 | tf_op jit(solution)/shard_map/ppermute | solution.py:23
  585.0 27.0 %collective-permute-start.8 = (bf16[4,16,6,128]{3,2,1,0:T(8,128)(2,1)S(1)}, bf16[4,16,6,128]{3,2,1,0:T(8,128)(2,1)S(1)}, u32[]{:S(2)}, u32[]{:S(2)}) collective-permute-start(bf16[4,16,6,128]{3,2,1,0:T(8,128)(2,1)S(1)} %get-tuple-element.8), channel_id=1, source_target_pairs={{0,128},{16,144},{32,160},{48,176},{64,192},{80,208},{96,224},{112... | collective-permute-start | bytes 294920 | tf_op jit(solution)/shard_map/ppermute | solution.py:23
  586.9 14.3 %collective-permute-start.10 = (bf16[4,16,16,6]{3,2,1,0:T(8,128)(2,1)S(1)}, bf16[4,16,16,6]{3,2,1,0:T(8,128)(2,1)S(1)}, u32[]{:S(2)}, u32[]{:S(2)}) collective-permute-start(bf16[4,16,16,6]{3,2,1,0:T(8,128)(2,1)S(1)} %get-tuple-element.12), channel_id=1, source_target_pairs={{0,32},{16,48},{32,0},{48,16},{64,96},{80,112},{96,64},{112,80},{1... | collective-permute-start | bytes 36872 | tf_op jit(solution)/shard_map/ppermute | solution.py:23
  591.2 20.7 %collective-permute-start.11 = (bf16[4,16,16,6]{3,2,1,0:T(8,128)(2,1)S(1)}, bf16[4,16,16,6]{3,2,1,0:T(8,128)(2,1)S(1)}, u32[]{:S(2)}, u32[]{:S(2)}) collective-permute-start(bf16[4,16,16,6]{3,2,1,0:T(8,128)(2,1)S(1)} %get-tuple-element.13), channel_id=1, source_target_pairs={{0,16},{16,0},{32,48},{48,32},{64,80},{80,64},{96,112},{112,96},{1... | collective-permute-start | bytes 36872 | tf_op jit(solution)/shard_map/ppermute | solution.py:23
  601.2 16.6 %collective-permute-start.9 = (bf16[4,16,6,128]{3,2,1,0:T(8,128)(2,1)S(1)}, bf16[4,16,6,128]{3,2,1,0:T(8,128)(2,1)S(1)}, u32[]{:S(2)}, u32[]{:S(2)}) collective-permute-start(bf16[4,16,6,128]{3,2,1,0:T(8,128)(2,1)S(1)} %get-tuple-element.9), channel_id=1, source_target_pairs={{0,64},{16,80},{32,96},{48,112},{64,0},{80,16},{96,32},{112,48},{1... | collective-permute-start | bytes 294920 | tf_op jit(solution)/shard_map/ppermute | solution.py:23
Sparse Core Ops, SparseCore 0:
  622.9 102.0 all-gather.2
where the time goes:
time: 879 us; the launch traced here: 875 us
  blocking collectives  639 us (73%)
  waiting for transfers between devices  113 us (13%)
  starting transfers between devices  65.8 us (7%)
  matrix products  22 us (3%)
  between operations  15.1 us (2%)
  other arithmetic  12.1 us (1%)
    psum x2, blocking collectives, project(): coefficient = lax.psum(local_coef, 'domain')  507 us
    psum x1, blocking collectives, on_device(): margin = lax.psum(product, 'domain') / total_cells  132 us
    all_gather x1, waiting for transfers between devices, on_device(): lax.all_gather(rounded, 'band', axis=0, tiled=True)  102 us
    ppermute x12, starting transfers between devices, from_partner(): return lax.ppermute(value, axis, pairs)  65.7 us
  transfers between devices with their start and end apart: 13, of which 3 were waited for; matrix products, arithmetic and copies ran while one was open for 2% of the time, Pallas kernels for 0%

commit v1 on v0

v1 whole, which is shorter than its diff:
```python
import jax
import jax.numpy as jnp
from jax import lax
from jax.experimental import pallas as pl
from jax.experimental.pallas import tpu as pltpu
from jax.sharding import PartitionSpec as P

STENCIL = (
    -5369.0 / 1800.0,
    12.0 / 7.0,
    -15.0 / 56.0,
    10.0 / 189.0,
    -1.0 / 112.0,
    2.0 / 1925.0,
    -1.0 / 16632.0,
)
SPACING = 0.5
CENTER = 27.5
HALF_WIDTH = 22.5
RADIUS = 6
ORBS = 4
SLOTS = 32
CELLROWS = 256
PADROWS = 448
LOW = 96
DOMAINS = 64
BANDS = 16
NCELLS = 2097152

SCALE = -0.5 / (SPACING * SPACING) / HALF_WIDTH
COEF = [SCALE * c for c in STENCIL]
MESH = pl.DeviceIdType.MESH


def neighbours(d):
    found = []
    for low in (16, 4, 1):
        first, second = d // low % 2, d // (2 * low) % 2
        by_first = d + low * (1 - 2 * first)
        by_second = d + 2 * low * (1 - 2 * second)
        lead = 1 - (first + second) % 2
        found.append(lead * by_first + (1 - lead) * by_second)
        found.append(lead * by_second + (1 - lead) * by_first)
    return found


def split(value):
    high = value.astype(jnp.bfloat16)
    low = (value - high.astype(jnp.float32)).astype(jnp.bfloat16)
    return high, low


def dot_nt(left, right):
    return lax.dot_general(
        left, right, (((1,), (1,)), ((), ())), preferred_element_type=jnp.float32
    )


def dot_tn(left, right):
    return lax.dot_general(
        left, right, (((0,), (0,)), ((), ())), preferred_element_type=jnp.float32
    )


def filter_kernel(
    ids_ref,
    count_ref,
    energies_ref,
    orb_ref,
    pot_ref,
    proj_ref,
    filt_ref,
    round_ref,
    field,
    turned,
    proj,
    proj_rows,
    diag,
    face_send,
    face_recv,
    edge_send,
    edge_recv,
    coef_send,
    coef_recv,
    band_matrix,
    edge_matrix,
    pick_matrix,
    selector,
    splat,
    term_y,
    term_z,
    in_sem,
    halo_send_sem,
    halo_recv_sem,
    coef_send_sem,
    coef_recv_sem,
):
    d = lax.axis_index("domain")
    b = lax.axis_index("band")
    near = neighbours(d)

    loads = [
        pltpu.make_async_copy(
            orb_ref.at[pl.ds(o * CELLROWS, CELLROWS)],
            field.at[0, o, pl.ds(LOW, CELLROWS)],
            in_sem.at[o],
        )
        for o in range(ORBS)
    ]
    loads.append(pltpu.make_async_copy(proj_ref, proj, in_sem.at[ORBS]))
    loads.append(pltpu.make_async_copy(pot_ref, diag, in_sem.at[ORBS + 1]))
    for load in loads:
        load.start()

    barrier = pltpu.get_barrier_semaphore()
    for k in range(6):
        pl.semaphore_signal(barrier, inc=1, device_id=(near[k], b), device_id_type=MESH)

    rows = lax.broadcasted_iota(jnp.int32, (128, 128), 0)
    lanes = lax.broadcasted_iota(jnp.int32, (128, 128), 1)
    apart = jnp.abs(rows - lanes)
    banded = jnp.zeros((128, 128), jnp.float32)
    for k in range(1, RADIUS + 1):
        banded = jnp.where(apart == k, COEF[k], banded)
    high, low = split(banded)
    band_matrix[0:128, 0:128] = high
    band_matrix[128:256, 0:128] = high
    band_matrix[0:128, 128:256] = low
    band_matrix[128:256, 128:256] = low

    rows = lax.broadcasted_iota(jnp.int32, (32, 128), 0)
    lanes = lax.broadcasted_iota(jnp.int32, (32, 128), 1)
    layer = rows & 7
    half = (rows >> 3) & 1
    side = rows >> 4
    used = layer < RADIUS
    reach = jnp.where(side == 0, lanes + RADIUS - layer, 128 + layer - lanes)
    edge = jnp.zeros((32, 128), jnp.float32)
    for k in range(1, RADIUS + 1):
        edge = jnp.where(reach == k, COEF[k], edge)
    edge = jnp.where(used, edge, 0.0)
    picked = jnp.where(side == 0, 128 - RADIUS + layer, layer)
    pick = jnp.where(used, jnp.where(lanes == picked, 1.0, 0.0), 0.0)
    for part in range(2):
        high, low = split(jnp.where(half == part, edge, 0.0))
        edge_matrix[:, 256 * part : 256 * part + 128] = high
        edge_matrix[:, 256 * part + 128 : 256 * part + 256] = low
        pick_matrix[:, 128 * part : 128 * part + 128] = jnp.where(half == part, pick, 0.0).astype(
            jnp.bfloat16
        )

    lane = lax.broadcasted_iota(jnp.int32, (1, 128), 1)
    group = lane >> 4
    target = jnp.full((1, 128), -(2**20), jnp.int32)
    for g, block in enumerate(near + [d]):
        target = jnp.where(group == g, block * 16 + (lane & 15), target)
    live = count_ref[0]
    for s in range(SLOTS):
        named = jnp.where(s < live, ids_ref[s], -1)
        selector[s : s + 1, :] = jnp.where(target == named, 1.0, 0.0)
    own_energy = energies_ref[pl.ds(d // 8, 1), :]
    own_energy = pltpu.roll(own_energy, (128 - d % 8 * 16) % 128, 1)
    own_energy = jnp.where(lane < 16, own_energy / HALF_WIDTH, 0.0)

    def halo_copy(h, o, k):
        if k < 4:
            src, dst = face_send.at[h, o, k], face_recv.at[h, o, k ^ 1]
        else:
            src, dst = edge_send.at[h, o, k - 4], edge_recv.at[h, o, (k ^ 1) - 4]
        return pltpu.make_async_remote_copy(
            src_ref=src,
            dst_ref=dst,
            send_sem=halo_send_sem.at[h, o, k],
            recv_sem=halo_recv_sem.at[h, o, k ^ 1],
            device_id=(near[k], b),
            device_id_type=MESH,
        )

    def send_halo(h, o):
        for k in range(6):
            halo_copy(h, o, k).start()

    def coef_copy(h, turn, k):
        return pltpu.make_async_remote_copy(
            src_ref=coef_send.at[h, turn],
            dst_ref=coef_recv.at[h, turn, k ^ 1],
            send_sem=coef_send_sem.at[h, turn, k],
            recv_sem=coef_recv_sem.at[h, turn, k ^ 1],
            device_id=(near[k], b),
            device_id_type=MESH,
        )

    def prepare(h, o):
        face_send[h, o, 0] = field[h, o, pl.ds(LOW + 160, LOW), :].astype(jnp.bfloat16)
        face_send[h, o, 1] = field[h, o, pl.ds(LOW, LOW), :].astype(jnp.bfloat16)
        for y in range(16):
            layer = field[h, o, pl.ds(LOW + y, 16, stride=16), :]
            turned[o, pl.ds(LOW + 16 * y, 16), :] = layer
            if y >= 10:
                face_send[h, o, 2, pl.ds(16 * (y - 10), 16), :] = layer.astype(jnp.bfloat16)
            if y < RADIUS:
                face_send[h, o, 3, pl.ds(16 * y, 16), :] = layer.astype(jnp.bfloat16)
        first_half = field[h, o, pl.ds(LOW, 128), :].astype(jnp.bfloat16)
        second_half = field[h, o, pl.ds(LOW + 128, 128), :].astype(jnp.bfloat16)
        edges = dot_nt(pick_matrix[:, 0:128], first_half) + dot_nt(
            pick_matrix[:, 128:256], second_half
        )
        edge_send[h, o, 0] = edges[0:16].astype(jnp.bfloat16)
        edge_send[h, o, 1] = edges[16:32].astype(jnp.bfloat16)

    def project(h):
        def body(x, sums):
            sums = list(sums)
            for y in range(16):
                row = x * 16 + y
                columns = proj[:, pl.ds(pl.multiple_of(row * 128, 128), 128)]
                for o in range(ORBS):
                    sums[o] = sums[o] + columns * field[h, o, pl.ds(LOW + row, 1), :]
            return tuple(sums)

        zero = jnp.zeros((SLOTS, 128), jnp.float32)
        sums = lax.fori_loop(0, 16, body, (zero,) * ORBS)
        chosen = selector[...]
        for o in range(ORBS):
            partial = jnp.sum(sums[o], axis=1, keepdims=True)
            coef_send[h, 0, o : o + 1, :] = jnp.sum(partial * chosen, axis=0, keepdims=True)
        for k in range(6):
            coef_copy(h, 0, k).start()

    def own_coefficients(h):
        for k in range(6):
            coef_copy(h, 0, k).wait_recv()
        total = pltpu.roll(coef_send[h, 0], 32, 1)
        for k in range(6):
            total = total + pltpu.roll(coef_recv[h, 0, k], (128 - 16 * (k ^ 1)) % 128, 1)
        coef_send[h, 1] = total * own_energy
        for k in range(6):
            coef_copy(h, 1, k).start()

    def weigh(h):
        for k in range(6):
            coef_copy(h, 1, k).wait_recv()
        known = pltpu.roll(coef_send[h, 1], 96, 1)
        for k in range(6):
            known = known + pltpu.roll(coef_recv[h, 1, k], 16 * k, 1)
        chosen = selector[...]
        for o in range(ORBS):
            weight = jnp.sum(chosen * known[o : o + 1, :], axis=1, keepdims=True)
            splat[o * SLOTS : (o + 1) * SLOTS, :] = jnp.broadcast_to(weight, (SLOTS, 128))

    def apply(h, o):
        for k in range(6):
            halo_copy(h, o, k).wait_recv()
        field[h, o, pl.ds(LOW + CELLROWS, LOW), :] = face_recv[h, o, 0].astype(jnp.float32)
        field[h, o, pl.ds(0, LOW), :] = face_recv[h, o, 1].astype(jnp.float32)
        turned[o, pl.ds(LOW + CELLROWS, LOW), :] = face_recv[h, o, 2].astype(jnp.float32)
        turned[o, pl.ds(0, LOW), :] = face_recv[h, o, 3].astype(jnp.float32)

        high, low = split(field[h, o, pl.ds(LOW, CELLROWS), :])
        along = jnp.dot(
            jnp.concatenate([high, low], axis=1),
            band_matrix[...],
            preferred_element_type=jnp.float32,
        )
        along = along[:, 0:128] + along[:, 128:256]
        ends = dot_tn(
            jnp.concatenate([edge_recv[h, o, 1], edge_recv[h, o, 0]], axis=0), edge_matrix[...]
        )
        term_z[0:128, :] = along[0:128] + (ends[:, 0:128] + ends[:, 128:256])
        term_z[128:256, :] = along[128:256] + (ends[:, 256:384] + ends[:, 384:512])

        def body_y(y, carry):
            total = jnp.zeros((64, 128), jnp.float32)
            for k in range(1, RADIUS + 1):
                total = total + COEF[k] * (
                    turned[o, pl.ds(LOW + 64 * y + 16 * k, 64), :]
                    + turned[o, pl.ds(LOW + 64 * y - 16 * k, 64), :]
                )
            term_y[pl.ds(64 * y, 64), :] = total
            return carry

        lax.fori_loop(0, 4, body_y, 0)

        def body_x(x, carry):
            here = pl.ds(64 * x, 64)
            value = field[h, o, pl.ds(LOW + 64 * x, 64), :]
            total = diag[here, :] * value + term_z[here, :]
            total = total + jnp.concatenate(
                [term_y[pl.ds(4 * x + i, 16, stride=16), :] for i in range(4)], axis=0
            )
            for k in range(1, RADIUS + 1):
                total = total + COEF[k] * (
                    field[h, o, pl.ds(LOW + 64 * x + 16 * k, 64), :]
                    + field[h, o, pl.ds(LOW + 64 * x - 16 * k, 64), :]
                )
            for s in range(SLOTS):
                total = total + splat[pl.ds(o * SLOTS + s, 1), :] * proj_rows[
                    pl.ds(s * CELLROWS + 64 * x, 64), :
                ]
            if h == 0:
                field[1, o, pl.ds(LOW + 64 * x, 64), :] = total
            else:
                total = 2.0 * total - field[0, o, pl.ds(LOW + 64 * x, 64), :]
                place = pl.ds(o * CELLROWS + 64 * x, 64)
                filt_ref[place, :] = total
                round_ref[place, :] = total.astype(jnp.bfloat16)
            return carry

        lax.fori_loop(0, 4, body_x, 0)

    def over_orbitals(body, first=0, last=ORBS):
        lax.fori_loop(first, last, lambda o, carry: (body(o), carry)[1], 0)

    for o in range(ORBS):
        loads[o].wait()
    over_orbitals(lambda o: prepare(0, o))
    pl.semaphore_wait(barrier, 6)
    send_halo(0, 0)
    loads[ORBS].wait()
    project(0)
    send_halo(0, 1)

    def turn(row, carry):
        proj_rows[pl.ds(row, SLOTS, stride=CELLROWS), :] = proj[
            :, pl.ds(pl.multiple_of(row * 128, 128), 128)
        ]
        return carry

    lax.fori_loop(0, CELLROWS, turn, 0, unroll=8)
    loads[ORBS + 1].wait()
    diag[...] = (diag[...] + (-0.5 / (SPACING * SPACING) * 3.0 * STENCIL[0] - CENTER)) * (
        1.0 / HALF_WIDTH
    )
    own_coefficients(0)
    send_halo(0, 2)
    send_halo(0, 3)
    weigh(0)

    def first_step(o):
        apply(0, o)
        prepare(1, o)

    def first_step_and_send(o):
        first_step(o)
        send_halo(1, o)

    over_orbitals(first_step_and_send, 0, 2)
    over_orbitals(first_step, 2, 4)
    project(1)
    send_halo(1, 2)
    own_coefficients(1)
    send_halo(1, 3)
    weigh(1)
    over_orbitals(lambda o: apply(1, o))

    for h in range(2):
        for turn_ in range(2):
            for k in range(6):
                coef_copy(h, turn_, k).wait_send()

        def sent(o):
            for k in range(6):
                halo_copy(h, o, k).wait_send()

        over_orbitals(sent)


def margin_kernel(
    round_ref,
    margin_ref,
    cells,
    wide,
    shares,
    gathered,
    group_low,
    group_high,
    cell_send_sem,
    cell_recv_sem,
    share_send_sem,
    share_recv_sem,
    low_send_sem,
    low_recv_sem,
    high_send_sem,
    high_recv_sem,
):
    d = lax.axis_index("domain")
    b = lax.axis_index("band")
    d_low, d_high = d % 8, d // 8

    def band_peer(i):
        return (b + i) % BANDS

    def low_peer(i):
        return d_high * 8 + (d_low + i) % 8

    def high_peer(i):
        return (d_high + i) % 8 * 8 + d_low

    def each(first, last, body):
        lax.fori_loop(first, last, lambda i, carry: (body(i), carry)[1], 0)

    barrier = pltpu.get_barrier_semaphore()

    def greet_band(i):
        pl.semaphore_signal(barrier, inc=1, device_id=(d, band_peer(i)), device_id_type=MESH)

    def greet_domain(i):
        pl.semaphore_signal(barrier, inc=1, device_id=(low_peer(i), b), device_id_type=MESH)
        pl.semaphore_signal(barrier, inc=1, device_id=(high_peer(i), b), device_id_type=MESH)

    each(1, BANDS, greet_band)
    each(1, 8, greet_domain)
    cells[b] = round_ref[:, b]
    pl.semaphore_wait(barrier, BANDS - 1 + 14)

    def cell_copy(i):
        return pltpu.make_async_remote_copy(
            src_ref=round_ref.at[:, band_peer(i)],
            dst_ref=cells.at[b],
            send_sem=cell_send_sem.at[i],
            recv_sem=cell_recv_sem.at[i],
            device_id=(d, band_peer(i)),
            device_id_type=MESH,
        )

    def share_copy(i):
        return pltpu.make_async_remote_copy(
            src_ref=shares.at[band_peer(i)],
            dst_ref=gathered.at[b],
            send_sem=share_send_sem.at[i],
            recv_sem=share_recv_sem.at[i],
            device_id=(d, band_peer(i)),
            device_id_type=MESH,
        )

    def low_copy(i):
        return pltpu.make_async_remote_copy(
            src_ref=group_low.at[d_low],
            dst_ref=group_low.at[d_low],
            send_sem=low_send_sem.at[i],
            recv_sem=low_recv_sem.at[i],
            device_id=(low_peer(i), b),
            device_id_type=MESH,
        )

    def high_copy(i):
        return pltpu.make_async_remote_copy(
            src_ref=group_high.at[d_high],
            dst_ref=group_high.at[d_high],
            send_sem=high_send_sem.at[i],
            recv_sem=high_recv_sem.at[i],
            device_id=(high_peer(i), b),
            device_id_type=MESH,
        )

    each(1, BANDS, lambda i: cell_copy(i).start())
    each(1, BANDS, lambda i: cell_copy(i).wait_recv())

    def widen(j, carry):
        for o in range(ORBS):
            wide[pl.ds(j * 64 + o * 16, 16), :] = cells[j, o].astype(jnp.float32)
        return carry

    lax.fori_loop(0, BANDS, widen, 0)
    gram = jnp.zeros((64, 64), jnp.float32)
    for row in range(0, 16, 2):
        part = jnp.concatenate(
            [wide[pl.ds(row + i, 64, stride=16), :] for i in range(2)], axis=1
        ).astype(jnp.bfloat16)
        gram = gram + dot_nt(part, part)
    gram = jnp.concatenate([gram, jnp.zeros((64, 64), jnp.float32)], axis=1)
    for j in range(BANDS):
        shares[j] = gram[ORBS * j : ORBS * (j + 1), :]
    each(1, BANDS, lambda i: share_copy(i).start())
    gathered[b] = shares[b]
    each(1, BANDS, lambda i: share_copy(i).wait_recv())
    total = gathered[0]
    for j in range(1, BANDS):
        total = total + gathered[j]
    group_low[d_low] = total
    each(1, 8, lambda i: low_copy(i).start())
    each(1, 8, lambda i: low_copy(i).wait_recv())
    total = group_low[0]
    for j in range(1, 8):
        total = total + group_low[j]
    group_high[d_high] = total
    each(1, 8, lambda i: high_copy(i).start())
    each(1, 8, lambda i: high_copy(i).wait_recv())
    total = group_high[0]
    for j in range(1, 8):
        total = total + group_high[j]
    margin_ref[...] = total[:, 0:64] * (1.0 / NCELLS)

    each(1, BANDS, lambda i: cell_copy(i).wait_send())
    each(1, BANDS, lambda i: share_copy(i).wait_send())
    each(1, 8, lambda i: low_copy(i).wait_send())
    each(1, 8, lambda i: high_copy(i).wait_send())


def on_device(orbitals, potential, projectors, slot_ids, slot_count, energies):
    vmem = pl.BlockSpec(memory_space=pltpu.VMEM)
    smem = pl.BlockSpec(memory_space=pltpu.SMEM)
    anywhere = pl.BlockSpec(memory_space=pl.ANY)
    filtered, rounded = pl.pallas_call(
        filter_kernel,
        out_shape=(
            jax.ShapeDtypeStruct((ORBS * CELLROWS, 128), jnp.float32),
            jax.ShapeDtypeStruct((ORBS * CELLROWS, 128), jnp.bfloat16),
        ),
        in_specs=[smem, smem, vmem, anywhere, anywhere, anywhere],
        out_specs=(vmem, vmem),
        scratch_shapes=[
            pltpu.VMEM((2, ORBS, PADROWS, 128), jnp.float32),
            pltpu.VMEM((ORBS, PADROWS, 128), jnp.float32),
            pltpu.VMEM((SLOTS, 32768), jnp.float32),
            pltpu.VMEM((SLOTS * CELLROWS, 128), jnp.float32),
            pltpu.VMEM((CELLROWS, 128), jnp.float32),
            pltpu.VMEM((2, ORBS, 4, LOW, 128), jnp.bfloat16),
            pltpu.VMEM((2, ORBS, 4, LOW, 128), jnp.bfloat16),
            pltpu.VMEM((2, ORBS, 2, 16, 128), jnp.bfloat16),
            pltpu.VMEM((2, ORBS, 2, 16, 128), jnp.bfloat16),
            pltpu.VMEM((2, 2, ORBS, 128), jnp.float32),
            pltpu.VMEM((2, 2, 6, ORBS, 128), jnp.float32),
            pltpu.VMEM((256, 256), jnp.bfloat16),
            pltpu.VMEM((32, 512), jnp.bfloat16),
            pltpu.VMEM((32, 256), jnp.bfloat16),
            pltpu.VMEM((SLOTS, 128), jnp.float32),
            pltpu.VMEM((ORBS * SLOTS, 128), jnp.float32),
            pltpu.VMEM((CELLROWS, 128), jnp.float32),
            pltpu.VMEM((CELLROWS, 128), jnp.float32),
            pltpu.SemaphoreType.DMA((ORBS + 2,)),
            pltpu.SemaphoreType.DMA((2, ORBS, 6)),
            pltpu.SemaphoreType.DMA((2, ORBS, 6)),
            pltpu.SemaphoreType.DMA((2, 2, 6)),
            pltpu.SemaphoreType.DMA((2, 2, 6)),
        ],
        compiler_params=pltpu.CompilerParams(
            collective_id=0, has_side_effects=True, vmem_limit_bytes=40 * 2**20
        ),
        name="filter",
    )(
        slot_ids,
        slot_count,
        energies.reshape(8, 128),
        orbitals.reshape(ORBS * CELLROWS, 128),
        potential.reshape(CELLROWS, 128),
        projectors,
    )
    margin = pl.pallas_call(
        margin_kernel,
        out_shape=jax.ShapeDtypeStruct((ORBS, 64), jnp.float32),
        in_specs=[vmem],
        out_specs=vmem,
        scratch_shapes=[
            pltpu.VMEM((BANDS, ORBS, 16, 128), jnp.bfloat16),
            pltpu.VMEM((64 * 16, 128), jnp.float32),
            pltpu.VMEM((BANDS, ORBS, 128), jnp.float32),
            pltpu.VMEM((BANDS, ORBS, 128), jnp.float32),
            pltpu.VMEM((8, ORBS, 128), jnp.float32),
            pltpu.VMEM((8, ORBS, 128), jnp.float32),
            pltpu.SemaphoreType.DMA((BANDS,)),
            pltpu.SemaphoreType.DMA((BANDS,)),
            pltpu.SemaphoreType.DMA((BANDS,)),
            pltpu.SemaphoreType.DMA((BANDS,)),
            pltpu.SemaphoreType.DMA((8,)),
            pltpu.SemaphoreType.DMA((8,)),
            pltpu.SemaphoreType.DMA((8,)),
            pltpu.SemaphoreType.DMA((8,)),
        ],
        compiler_params=pltpu.CompilerParams(
            collective_id=1, has_side_effects=True, vmem_limit_bytes=16 * 2**20
        ),
        name="margin",
    )(rounded.reshape(ORBS, BANDS, 16, 128))
    return filtered.reshape(orbitals.shape), margin


def solution(mesh):
    in_specs = (
        P("band", "domain", None, None),
        P("domain", None, None),
        P("domain", None),
        P("domain"),
        P("domain"),
        P(),
    )
    out_specs = (P("band", "domain", None, None), P("band", None))
    return jax.shard_map(
        on_device, mesh=mesh, in_specs=in_specs, out_specs=out_specs, check_vma=False
    )
```

time: 879 us -> 114 us (0.13)
  blocking collectives: 639 us -> 0 us
  waiting for transfers between devices: 113 us -> 0 us
  Pallas kernels: 0 us -> 106 us
  starting transfers between devices: 65.8 us -> 0 us
  matrix products: 22 us -> 0 us
  between operations: 15.1 us -> 1.31 us
  other arithmetic: 12.1 us -> 0 us
    psum x3 -> x0, blocking collectives: 639 us -> none  [the longest x2 507 us: project(): coefficient = lax.psum(local_coef, 'domain')]
    pallas_call x0 -> x2, Pallas kernels: none -> 106 us  [the longest x1 64.1 us: on_device(): pl.pallas_call(filter_kernel, out_shape=(jax.ShapeDtypeStruct((ORBS * CEL...]
    all_gather x1 -> x0, waiting for transfers between devices: 102 us -> none  [on_device(): lax.all_gather(rounded, 'band', axis=0, tiled=True)]
    ppermute x12 -> x0, starting transfers between devices: 65.7 us -> none  [from_partner(): return lax.ppermute(value, axis, pairs)]
    dot_general x9 -> x0, matrix products: 22 us -> none  [the longest x2 9.12 us: contract_cells(): lax.dot_general(left_side, right_side, (((1,), (1,)), ((), ())), precisio...]
    ppermute x12 -> x0, waiting for transfers between devices: 10.4 us -> none  [from_partner(): return lax.ppermute(value, axis, pairs)]
  transfers between devices with their start and end apart: 13 -> 0, of which waited for: 3 -> 0; matrix products, arithmetic and copies ran while one was open for 2% -> 0% of each run, Pallas kernels for 0% -> 0%
where the time goes in v1:
time: 114 us
  Pallas kernels  106 us (93%)
  local copies, waits for them, and re-layouts  6.84 us (6%)
  between operations  1.31 us (1%)
    pallas_call x1, Pallas kernels, on_device(): pl.pallas_call(filter_kernel, out_shape=(jax.ShapeDtypeStruct((ORBS * CEL...  64.1 us
    pallas_call x1, Pallas kernels, on_device(): pl.pallas_call(margin_kernel, out_shape=jax.ShapeDtypeStruct((ORBS, 64),...  41.4 us
    unnamed x12, local copies, waits for them, and re-layouts  6.84 us

profile of v1, /device:TPU:1, one launch (start us, length us, event | category | flops | bytes accessed | tf_op | source)
XLA Modules:
  0.0 113.6 jit_solution(12966309384614581254)
XLA Ops:
  1.3 0.0 copy-start
  1.3 2.2 %copy-done = f32[32,32768]{1,0:T(8,128)S(1)} copy-done((f32[32,32768]{1,0:T(8,128)S(1)}, f32[32,32768]{1,0:T(8,128)}, u32[]{:S(2)}) %copy-start) | copy-done | bytes 4194328
  3.5 0.0 copy-start.1
  3.5 1.0 copy-done.1
  4.5 0.0 copy-start.2
  4.5 0.9 copy-done.2
  5.4 0.0 copy-start.3
  5.4 0.7 copy-done.3
  6.1 0.0 copy-start.4
  6.1 0.7 copy-done.4
  6.8 64.1 %filter.1 = (f32[1024,128]{1,0:T(8,128)S(1)}, bf16[1024,128]{1,0:T(8,128)(2,1)S(1)}) custom-call(s32[32]{0:T(128)S(1)} %copy-done.4, s32[1]{0:T(128)S(6)} %copy.10.count_ref, f32[8,128]{1,0:T(8,128)S(1)} %bitcast.9, f32[1024,128]{1,0:T(8,128)S(1)} %bitcast.5, f32[256,128]{1,0:T(8,128)S(1)} %bitcast.8, f32[32,32768]{1,0:T(8,128)S(1)} %copy-done), custom_call_target="tpu_custom_call" | custom-call | tf_op jit(solution)/shard_map/filter/pallas_call | solution.py:504
  70.8 41.4 %margin.1 = f32[4,64]{1,0:T(4,128)S(1)} custom-call(bf16[4,16,16,128]{3,2,1,0:T(8,128)(2,1)S(1)} %bitcast.7), custom_call_target="tpu_custom_call" | custom-call | tf_op jit(solution)/shard_map/margin/pallas_call | solution.py:549
  112.3 0.8 copy.11
  113.1 0.6 copy.12
Async XLA Ops:
  1.3 2.2 %copy-start = (f32[32,32768]{1,0:T(8,128)S(1)}, f32[32,32768]{1,0:T(8,128)}, u32[]{:S(2)}) copy-start(f32[32,32768]{1,0:T(8,128)} %proj_ref.1) | copy-start | bytes 12582916
  3.5 1.0 copy-start.1
  4.5 0.9 copy-start.2
  5.4 0.7 copy-start.3
  6.1 0.7 copy-start.4

commit v2 on v1

--- a/solution.py
+++ b/solution.py
@@ -62,15 +62,16 @@
     )
 
 
-def filter_kernel(
+def kernel(
     ids_ref,
     count_ref,
-    energies_ref,
+    energies_hbm,
     orb_ref,
     pot_ref,
     proj_ref,
-    filt_ref,
-    round_ref,
+    filt_hbm,
+    margin_ref,
+    energies_ref,
     field,
     turned,
     proj,
@@ -89,11 +90,28 @@
     splat,
     term_y,
     term_z,
+    filtered,
+    rounded,
+    cells,
+    wide,
+    shares,
+    gathered,
+    group_low,
+    group_high,
     in_sem,
+    out_sem,
     halo_send_sem,
     halo_recv_sem,
     coef_send_sem,
     coef_recv_sem,
+    cell_send_sem,
+    cell_recv_sem,
+    share_send_sem,
+    share_recv_sem,
+    low_send_sem,
+    low_recv_sem,
+    high_send_sem,
+    high_recv_sem,
 ):
     d = lax.axis_index("domain")
     b = lax.axis_index("band")
@@ -109,12 +127,35 @@
     ]
     loads.append(pltpu.make_async_copy(proj_ref, proj, in_sem.at[ORBS]))
     loads.append(pltpu.make_async_copy(pot_ref, diag, in_sem.at[ORBS + 1]))
+    loads.append(pltpu.make_async_copy(energies_hbm, energies_ref, in_sem.at[ORBS + 2]))
+
+    d_low, d_high = d % 8, d // 8
+
+    def band_peer(i):
+        return (b + i) % BANDS
+
+    def low_peer(i):
+        return d_high * 8 + (d_low + i) % 8
+
+    def high_peer(i):
+        return (d_high + i) % 8 * 8 + d_low
+
+    def each(first, last, body):
+        lax.fori_loop(first, last, lambda i, carry: (body(i), carry)[1], 0)
+
+    barrier = pltpu.get_barrier_semaphore()
+
+    def greet_band(i):
+        pl.semaphore_signal(barrier, inc=1, device_id=(d, band_peer(i)), device_id_type=MESH)
+
+    def greet_domain(i):
+        pl.semaphore_signal(barrier, inc=1, device_id=(high_peer(i), b), device_id_type=MESH)
+        pl.semaphore_signal(barrier, inc=1, device_id=(low_peer(i), b), device_id_type=MESH)
+
+    each(1, 8, greet_domain)
+    each(1, BANDS, greet_band)
     for load in loads:
         load.start()
-
-    barrier = pltpu.get_barrier_semaphore()
-    for k in range(6):
-        pl.semaphore_signal(barrier, inc=1, device_id=(near[k], b), device_id_type=MESH)
 
     rows = lax.broadcasted_iota(jnp.int32, (128, 128), 0)
     lanes = lax.broadcasted_iota(jnp.int32, (128, 128), 1)
@@ -158,6 +199,7 @@
     for s in range(SLOTS):
         named = jnp.where(s < live, ids_ref[s], -1)
         selector[s : s + 1, :] = jnp.where(target == named, 1.0, 0.0)
+    loads[ORBS + 2].wait()
     own_energy = energies_ref[pl.ds(d // 8, 1), :]
     own_energy = pltpu.roll(own_energy, (128 - d % 8 * 16) % 128, 1)
     own_energy = jnp.where(lane < 16, own_energy / HALF_WIDTH, 0.0)
@@ -180,12 +222,12 @@
         for k in range(6):
             halo_copy(h, o, k).start()
 
-    def coef_copy(h, turn, k):
+    def coef_copy(batch, turn, k):
         return pltpu.make_async_remote_copy(
-            src_ref=coef_send.at[h, turn],
-            dst_ref=coef_recv.at[h, turn, k ^ 1],
-            send_sem=coef_send_sem.at[h, turn, k],
-            recv_sem=coef_recv_sem.at[h, turn, k ^ 1],
+            src_ref=coef_send.at[batch, turn],
+            dst_ref=coef_recv.at[batch, turn, k ^ 1],
+            send_sem=coef_send_sem.at[batch, turn, k],
+            recv_sem=coef_recv_sem.at[batch, turn, k ^ 1],
             device_id=(near[k], b),
             device_id_type=MESH,
         )
@@ -208,49 +250,54 @@
         edge_send[h, o, 0] = edges[0:16].astype(jnp.bfloat16)
         edge_send[h, o, 1] = edges[16:32].astype(jnp.bfloat16)
 
-    def project(h):
+    def project(batch, h, orbs):
         def body(x, sums):
             sums = list(sums)
             for y in range(16):
                 row = x * 16 + y
                 columns = proj[:, pl.ds(pl.multiple_of(row * 128, 128), 128)]
-                for o in range(ORBS):
-                    sums[o] = sums[o] + columns * field[h, o, pl.ds(LOW + row, 1), :]
+                for i, o in enumerate(orbs):
+                    sums[i] = sums[i] + columns * field[h, o, pl.ds(LOW + row, 1), :]
             return tuple(sums)
 
         zero = jnp.zeros((SLOTS, 128), jnp.float32)
-        sums = lax.fori_loop(0, 16, body, (zero,) * ORBS)
+        sums = lax.fori_loop(0, 16, body, (zero,) * len(orbs))
         chosen = selector[...]
-        for o in range(ORBS):
-            partial = jnp.sum(sums[o], axis=1, keepdims=True)
-            coef_send[h, 0, o : o + 1, :] = jnp.sum(partial * chosen, axis=0, keepdims=True)
-        for k in range(6):
-            coef_copy(h, 0, k).start()
-
-    def own_coefficients(h):
-        for k in range(6):
-            coef_copy(h, 0, k).wait_recv()
-        total = pltpu.roll(coef_send[h, 0], 32, 1)
-        for k in range(6):
-            total = total + pltpu.roll(coef_recv[h, 0, k], (128 - 16 * (k ^ 1)) % 128, 1)
-        coef_send[h, 1] = total * own_energy
-        for k in range(6):
-            coef_copy(h, 1, k).start()
-
-    def weigh(h):
-        for k in range(6):
-            coef_copy(h, 1, k).wait_recv()
-        known = pltpu.roll(coef_send[h, 1], 96, 1)
-        for k in range(6):
-            known = known + pltpu.roll(coef_recv[h, 1, k], 16 * k, 1)
+        if len(orbs) < ORBS:
+            coef_send[batch, 0] = jnp.zeros((ORBS, 128), jnp.float32)
+        for i, o in enumerate(orbs):
+            partial = jnp.sum(sums[i], axis=1, keepdims=True)
+            coef_send[batch, 0, o : o + 1, :] = jnp.sum(partial * chosen, axis=0, keepdims=True)
+
+    def send_coefficients(batch, turn):
+        for k in range(6):
+            coef_copy(batch, turn, k).start()
+
+    def own_coefficients(batch):
+        for k in range(6):
+            coef_copy(batch, 0, k).wait_recv()
+        total = pltpu.roll(coef_send[batch, 0], 32, 1)
+        for k in range(6):
+            total = total + pltpu.roll(coef_recv[batch, 0, k], (128 - 16 * (k ^ 1)) % 128, 1)
+        coef_send[batch, 1] = total * own_energy
+        send_coefficients(batch, 1)
+
+    def weigh(batch, orbs):
+        for k in range(6):
+            coef_copy(batch, 1, k).wait_recv()
+        known = pltpu.roll(coef_send[batch, 1], 96, 1)
+        for k in range(6):
+            known = known + pltpu.roll(coef_recv[batch, 1, k], 16 * k, 1)
         chosen = selector[...]
-        for o in range(ORBS):
+        for o in orbs:
             weight = jnp.sum(chosen * known[o : o + 1, :], axis=1, keepdims=True)
             splat[o * SLOTS : (o + 1) * SLOTS, :] = jnp.broadcast_to(weight, (SLOTS, 128))
 
+    def receive(h, o):
+        for k in range(6):
+            halo_copy(h, o, k).wait_recv()
+
     def apply(h, o):
-        for k in range(6):
-            halo_copy(h, o, k).wait_recv()
         field[h, o, pl.ds(LOW + CELLROWS, LOW), :] = face_recv[h, o, 0].astype(jnp.float32)
         field[h, o, pl.ds(0, LOW), :] = face_recv[h, o, 1].astype(jnp.float32)
         turned[o, pl.ds(LOW + CELLROWS, LOW), :] = face_recv[h, o, 2].astype(jnp.float32)
@@ -302,126 +349,35 @@
             else:
                 total = 2.0 * total - field[0, o, pl.ds(LOW + 64 * x, 64), :]
                 place = pl.ds(o * CELLROWS + 64 * x, 64)
-                filt_ref[place, :] = total
-                round_ref[place, :] = total.astype(jnp.bfloat16)
+                filtered[place, :] = total
+                for i in range(4):
+                    rounded[o, 4 * x + i] = total[16 * i : 16 * i + 16].astype(jnp.bfloat16)
             return carry
 
         lax.fori_loop(0, 4, body_x, 0)
 
-    def over_orbitals(body, first=0, last=ORBS):
-        lax.fori_loop(first, last, lambda o, carry: (body(o), carry)[1], 0)
-
-    for o in range(ORBS):
-        loads[o].wait()
-    over_orbitals(lambda o: prepare(0, o))
-    pl.semaphore_wait(barrier, 6)
-    send_halo(0, 0)
-    loads[ORBS].wait()
-    project(0)
-    send_halo(0, 1)
-
-    def turn(row, carry):
-        proj_rows[pl.ds(row, SLOTS, stride=CELLROWS), :] = proj[
-            :, pl.ds(pl.multiple_of(row * 128, 128), 128)
-        ]
-        return carry
-
-    lax.fori_loop(0, CELLROWS, turn, 0, unroll=8)
-    loads[ORBS + 1].wait()
-    diag[...] = (diag[...] + (-0.5 / (SPACING * SPACING) * 3.0 * STENCIL[0] - CENTER)) * (
-        1.0 / HALF_WIDTH
-    )
-    own_coefficients(0)
-    send_halo(0, 2)
-    send_halo(0, 3)
-    weigh(0)
-
-    def first_step(o):
-        apply(0, o)
-        prepare(1, o)
-
-    def first_step_and_send(o):
-        first_step(o)
-        send_halo(1, o)
-
-    over_orbitals(first_step_and_send, 0, 2)
-    over_orbitals(first_step, 2, 4)
-    project(1)
-    send_halo(1, 2)
-    own_coefficients(1)
-    send_halo(1, 3)
-    weigh(1)
-    over_orbitals(lambda o: apply(1, o))
-
-    for h in range(2):
-        for turn_ in range(2):
-            for k in range(6):
-                coef_copy(h, turn_, k).wait_send()
-
-        def sent(o):
-            for k in range(6):
-                halo_copy(h, o, k).wait_send()
-
-        over_orbitals(sent)
-
-
-def margin_kernel(
-    round_ref,
-    margin_ref,
-    cells,
-    wide,
-    shares,
-    gathered,
-    group_low,
-    group_high,
-    cell_send_sem,
-    cell_recv_sem,
-    share_send_sem,
-    share_recv_sem,
-    low_send_sem,
-    low_recv_sem,
-    high_send_sem,
-    high_recv_sem,
-):
-    d = lax.axis_index("domain")
-    b = lax.axis_index("band")
-    d_low, d_high = d % 8, d // 8
-
-    def band_peer(i):
-        return (b + i) % BANDS
-
-    def low_peer(i):
-        return d_high * 8 + (d_low + i) % 8
-
-    def high_peer(i):
-        return (d_high + i) % 8 * 8 + d_low
-
-    def each(first, last, body):
-        lax.fori_loop(first, last, lambda i, carry: (body(i), carry)[1], 0)
-
-    barrier = pltpu.get_barrier_semaphore()
-
-    def greet_band(i):
-        pl.semaphore_signal(barrier, inc=1, device_id=(d, band_peer(i)), device_id_type=MESH)
-
-    def greet_domain(i):
-        pl.semaphore_signal(barrier, inc=1, device_id=(low_peer(i), b), device_id_type=MESH)
-        pl.semaphore_signal(barrier, inc=1, device_id=(high_peer(i), b), device_id_type=MESH)
-
-    each(1, BANDS, greet_band)
-    each(1, 8, greet_domain)
-    cells[b] = round_ref[:, b]
-    pl.semaphore_wait(barrier, BANDS - 1 + 14)
-
-    def cell_copy(i):
+    def part_of(part):
+        return (0, 2) if part == 0 else (part + 1, 1)
+
+    def result_copy(part):
+        first, many = part_of(part)
+        place = pl.ds(first * CELLROWS, many * CELLROWS)
+        return pltpu.make_async_copy(filtered.at[place], filt_hbm.at[place], out_sem.at[part])
+
+    def cell_copy(part, i):
+        orbs = pl.ds(*part_of(part))
         return pltpu.make_async_remote_copy(
-            src_ref=round_ref.at[:, band_peer(i)],
-            dst_ref=cells.at[b],
-            send_sem=cell_send_sem.at[i],
-            recv_sem=cell_recv_sem.at[i],
+            src_ref=rounded.at[orbs, band_peer(i)],
+            dst_ref=cells.at[b, orbs],
+            send_sem=cell_send_sem.at[part, i],
+            recv_sem=cell_recv_sem.at[part, i],
             device_id=(d, band_peer(i)),
             device_id_type=MESH,
         )
+
+    def publish(part):
+        each(1, BANDS, lambda i: cell_copy(part, i).start())
+        result_copy(part).start()
 
     def share_copy(i):
         return pltpu.make_async_remote_copy(
@@ -453,15 +409,73 @@
             device_id_type=MESH,
         )
 
-    each(1, BANDS, lambda i: cell_copy(i).start())
-    each(1, BANDS, lambda i: cell_copy(i).wait_recv())
-
-    def widen(j, carry):
+    for o in range(ORBS):
+        loads[o].wait()
+    each(0, ORBS, lambda o: prepare(0, o))
+    loads[ORBS].wait()
+    project(0, 0, (0, 1, 2, 3))
+    pl.semaphore_wait(barrier, 14 + BANDS - 1)
+    send_coefficients(0, 0)
+    send_halo(0, 0)
+    def turn(row, carry):
+        proj_rows[pl.ds(row, SLOTS, stride=CELLROWS), :] = proj[
+            :, pl.ds(pl.multiple_of(row * 128, 128), 128)
+        ]
+        return carry
+
+    lax.fori_loop(0, CELLROWS, turn, 0, unroll=8)
+    loads[ORBS + 1].wait()
+    diag[...] = (diag[...] + (-0.5 / (SPACING * SPACING) * 3.0 * STENCIL[0] - CENTER)) * (
+        1.0 / HALF_WIDTH
+    )
+    own_coefficients(0)
+    send_halo(0, 1)
+    receive(0, 0)
+    send_halo(0, 2)
+    weigh(0, (0, 1, 2, 3))
+
+    def first_step(o):
+        apply(0, o)
+        prepare(1, o)
+
+    first_step(0)
+    receive(0, 1)
+    send_halo(0, 3)
+    first_step(1)
+    receive(0, 2)
+    send_halo(1, 0)
+    first_step(2)
+    receive(0, 3)
+    first_step(3)
+    project(1, 1, (0, 1, 2, 3))
+    send_coefficients(1, 0)
+    send_halo(1, 1)
+
+    receive(1, 0)
+    send_halo(1, 2)
+    own_coefficients(1)
+    receive(1, 1)
+    send_halo(1, 3)
+    weigh(1, (0, 1, 2, 3))
+    apply(1, 0)
+    apply(1, 1)
+    publish(0)
+    receive(1, 2)
+    apply(1, 2)
+    publish(1)
+    receive(1, 3)
+    apply(1, 3)
+    publish(2)
+
+    cells[b] = rounded[:, b]
+    for part in range(3):
+        each(1, BANDS, lambda i: cell_copy(part, i).wait_recv())
+
+    def widen(j):
         for o in range(ORBS):
             wide[pl.ds(j * 64 + o * 16, 16), :] = cells[j, o].astype(jnp.float32)
-        return carry
-
-    lax.fori_loop(0, BANDS, widen, 0)
+
+    each(0, BANDS, widen)
     gram = jnp.zeros((64, 64), jnp.float32)
     for row in range(0, 16, 2):
         part = jnp.concatenate(
@@ -491,25 +505,44 @@
         total = total + group_high[j]
     margin_ref[...] = total[:, 0:64] * (1.0 / NCELLS)
 
-    each(1, BANDS, lambda i: cell_copy(i).wait_send())
+    for batch in range(2):
+        for turn_ in range(2):
+            for k in range(6):
+                coef_copy(batch, turn_, k).wait_send()
+
+    def sent(i):
+        for k in range(6):
+            halo_copy(i // ORBS, i % ORBS, k).wait_send()
+
+    each(0, 2 * ORBS, sent)
+    for part in range(3):
+        result_copy(part).wait()
+        each(1, BANDS, lambda i: cell_copy(part, i).wait_send())
     each(1, BANDS, lambda i: share_copy(i).wait_send())
     each(1, 8, lambda i: low_copy(i).wait_send())
     each(1, 8, lambda i: high_copy(i).wait_send())
 
 
+def copy_kernel(filt_in, margin_in, filt_out, margin_out):
+    filt_out[...] = filt_in[...]
+    margin_out[...] = margin_in[...]
+
+
 def on_device(orbitals, potential, projectors, slot_ids, slot_count, energies):
     vmem = pl.BlockSpec(memory_space=pltpu.VMEM)
     smem = pl.BlockSpec(memory_space=pltpu.SMEM)
-    anywhere = pl.BlockSpec(memory_space=pl.ANY)
-    filtered, rounded = pl.pallas_call(
-        filter_kernel,
+    hbm = pl.BlockSpec(memory_space=pltpu.HBM)
+    dma = pltpu.SemaphoreType.DMA
+    filtered, margin = pl.pallas_call(
+        kernel,
         out_shape=(
             jax.ShapeDtypeStruct((ORBS * CELLROWS, 128), jnp.float32),
-            jax.ShapeDtypeStruct((ORBS * CELLROWS, 128), jnp.bfloat16),
+            jax.ShapeDtypeStruct((ORBS, 64), jnp.float32),
         ),
-        in_specs=[smem, smem, vmem, anywhere, anywhere, anywhere],
-        out_specs=(vmem, vmem),
+        in_specs=[smem, smem] + [hbm] * 4,
+        out_specs=(hbm, vmem),
         scratch_shapes=[
+            pltpu.VMEM((8, 128), jnp.float32),
             pltpu.VMEM((2, ORBS, PADROWS, 128), jnp.float32),
             pltpu.VMEM((ORBS, PADROWS, 128), jnp.float32),
             pltpu.VMEM((SLOTS, 32768), jnp.float32),
@@ -528,16 +561,33 @@
             pltpu.VMEM((ORBS * SLOTS, 128), jnp.float32),
             pltpu.VMEM((CELLROWS, 128), jnp.float32),
             pltpu.VMEM((CELLROWS, 128), jnp.float32),
-            pltpu.SemaphoreType.DMA((ORBS + 2,)),
-            pltpu.SemaphoreType.DMA((2, ORBS, 6)),
-            pltpu.SemaphoreType.DMA((2, ORBS, 6)),
-            pltpu.SemaphoreType.DMA((2, 2, 6)),
-            pltpu.SemaphoreType.DMA((2, 2, 6)),
+            pltpu.VMEM((ORBS * CELLROWS, 128), jnp.float32),
+            pltpu.VMEM((ORBS, BANDS, 16, 128), jnp.bfloat16),
+            pltpu.VMEM((BANDS, ORBS, 16, 128), jnp.bfloat16),
+            pltpu.VMEM((64 * 16, 128), jnp.float32),
+            pltpu.VMEM((BANDS, ORBS, 128), jnp.float32),
+            pltpu.VMEM((BANDS, ORBS, 128), jnp.float32),
+            pltpu.VMEM((8, ORBS, 128), jnp.float32),
+            pltpu.VMEM((8, ORBS, 128), jnp.float32),
+            dma((ORBS + 3,)),
+            dma((3,)),
+            dma((2, ORBS, 6)),
+            dma((2, ORBS, 6)),
+            dma((2, 2, 6)),
+            dma((2, 2, 6)),
+            dma((3, BANDS)),
+            dma((3, BANDS)),
+            dma((BANDS,)),
+            dma((BANDS,)),
+            dma((8,)),
+            dma((8,)),
+            dma((8,)),
+            dma((8,)),
         ],
         compiler_params=pltpu.CompilerParams(
-            collective_id=0, has_side_effects=True, vmem_limit_bytes=40 * 2**20
+            collective_id=0, has_side_effects=True, vmem_limit_bytes=62 * 2**20
         ),
-        name="filter",
+        name="chebyshev",
     )(
         slot_ids,
         slot_count,
@@ -546,32 +596,16 @@
         potential.reshape(CELLROWS, 128),
         projectors,
     )
-    margin = pl.pallas_call(
-        margin_kernel,
-        out_shape=jax.ShapeDtypeStruct((ORBS, 64), jnp.float32),
-        in_specs=[vmem],
-        out_specs=vmem,
-        scratch_shapes=[
-            pltpu.VMEM((BANDS, ORBS, 16, 128), jnp.bfloat16),
-            pltpu.VMEM((64 * 16, 128), jnp.float32),
-            pltpu.VMEM((BANDS, ORBS, 128), jnp.float32),
-            pltpu.VMEM((BANDS, ORBS, 128), jnp.float32),
-            pltpu.VMEM((8, ORBS, 128), jnp.float32),
-            pltpu.VMEM((8, ORBS, 128), jnp.float32),
-            pltpu.SemaphoreType.DMA((BANDS,)),
-            pltpu.SemaphoreType.DMA((BANDS,)),
-            pltpu.SemaphoreType.DMA((BANDS,)),
-            pltpu.SemaphoreType.DMA((BANDS,)),
-            pltpu.SemaphoreType.DMA((8,)),
-            pltpu.SemaphoreType.DMA((8,)),
-            pltpu.SemaphoreType.DMA((8,)),
-            pltpu.SemaphoreType.DMA((8,)),
-        ],
-        compiler_params=pltpu.CompilerParams(
-            collective_id=1, has_side_effects=True, vmem_limit_bytes=16 * 2**20
+    filtered, margin = pl.pallas_call(
+        copy_kernel,
+        out_shape=(
+            jax.ShapeDtypeStruct(filtered.shape, jnp.float32),
+            jax.ShapeDtypeStruct(margin.shape, jnp.float32),
         ),
-        name="margin",
-    )(rounded.reshape(ORBS, BANDS, 16, 128))
+        in_specs=[vmem, vmem],
+        out_specs=(vmem, vmem),
+        name="results",
+    )(filtered, margin)
     return filtered.reshape(orbitals.shape), margin
 
 

time: 114 us -> 102 us (0.89)
  local copies, waits for them, and re-layouts: 6.84 us -> 0 us
  Pallas kernels: 106 us -> 101 us
    unnamed x12 -> x0, local copies, waits for them, and re-layouts: 6.84 us -> none
    pallas_call x2, Pallas kernels: 106 us -> 101 us  [the longest x1 99 us: on_device(): pl.pallas_call(kernel, out_shape=(jax.ShapeDtypeStruct((ORBS * CELLROWS,...]
where the time goes in v2:
time: 102 us
  Pallas kernels  101 us (99%)
  between operations  1.29 us (1%)
    pallas_call x1, Pallas kernels, on_device(): pl.pallas_call(kernel, out_shape=(jax.ShapeDtypeStruct((ORBS * CELLROWS,...  99 us

profile of v2, /device:TPU:1, one launch (start us, length us, event | category | flops | bytes accessed | tf_op | source)
XLA Modules:
  0.0 102.2 jit_solution(14484462483147244184)
XLA Ops:
  1.3 99.0 %chebyshev.1 = (f32[1024,128]{1,0:T(8,128)}, f32[4,64]{1,0:T(4,128)}) custom-call(s32[32]{0:T(128)} %ids_ref.1, s32[1]{0:T(128)S(6)} %copy.8.count_ref, f32[8,128]{1,0:T(8,128)} %bitcast.6, f32[1024,128]{1,0:T(8,128)} %bitcast.4, f32[256,128]{1,0:T(8,128)} %bitcast.5, f32[32,32768]{1,0:T(8,128)} %proj_ref.1), custom_call_target="tpu_custom_call" | custom-call | tf_op jit(solution)/shard_map/chebyshev/pallas_call | solution.py:536
  100.3 1.9 %results.1 = (f32[1024,128]{1,0:T(8,128)}, f32[4,64]{1,0:T(4,128)}) custom-call(f32[1024,128]{1,0:T(8,128)} %get-tuple-element.6.filt_in, f32[4,64]{1,0:T(4,128)} %get-tuple-element.7.margin_in), custom_call_target="tpu_custom_call" | custom-call | tf_op jit(solution)/shard_map/results/pallas_call | solution.py:599

commit v3 on v2

--- a/solution.py
+++ b/solution.py
@@ -44,6 +44,18 @@
     return found
 
 
+NEAR = (16, 32, 8, 4, 2, 1)
+AROUND = (24, 20, 18, 17, 40, 36, 34, 33, 48, 10, 9, 12, 6, 5, 3) + NEAR
+OTHERS = tuple(m for m in AROUND if m > 7 and m % 8)
+
+
+def flip(d, mask):
+    for bit in (1, 2, 4, 8, 16, 32):
+        if mask & bit:
+            d = d + bit * (1 - 2 * (d // bit % 2))
+    return d
+
+
 def split(value):
     high = value.astype(jnp.bfloat16)
     low = (value - high.astype(jnp.float32)).astype(jnp.bfloat16)
@@ -65,13 +77,12 @@
 def kernel(
     ids_ref,
     count_ref,
-    energies_hbm,
+    energies_ref,
     orb_ref,
     pot_ref,
     proj_ref,
     filt_hbm,
     margin_ref,
-    energies_ref,
     field,
     turned,
     proj,
@@ -86,7 +97,8 @@
     band_matrix,
     edge_matrix,
     pick_matrix,
-    selector,
+    down,
+    strength,
     splat,
     term_y,
     term_z,
@@ -127,7 +139,6 @@
     ]
     loads.append(pltpu.make_async_copy(proj_ref, proj, in_sem.at[ORBS]))
     loads.append(pltpu.make_async_copy(pot_ref, diag, in_sem.at[ORBS + 1]))
-    loads.append(pltpu.make_async_copy(energies_hbm, energies_ref, in_sem.at[ORBS + 2]))
 
     d_low, d_high = d % 8, d // 8
 
@@ -153,6 +164,8 @@
         pl.semaphore_signal(barrier, inc=1, device_id=(low_peer(i), b), device_id_type=MESH)
 
     each(1, 8, greet_domain)
+    for mask in OTHERS:
+        pl.semaphore_signal(barrier, inc=1, device_id=(flip(d, mask), b), device_id_type=MESH)
     each(1, BANDS, greet_band)
     for load in loads:
         load.start()
@@ -191,18 +204,16 @@
         )
 
     lane = lax.broadcasted_iota(jnp.int32, (1, 128), 1)
-    group = lane >> 4
-    target = jnp.full((1, 128), -(2**20), jnp.int32)
-    for g, block in enumerate(near + [d]):
-        target = jnp.where(group == g, block * 16 + (lane & 15), target)
     live = count_ref[0]
+    across = jnp.zeros((1, 128), jnp.float32)
     for s in range(SLOTS):
-        named = jnp.where(s < live, ids_ref[s], -1)
-        selector[s : s + 1, :] = jnp.where(target == named, 1.0, 0.0)
-    loads[ORBS + 2].wait()
-    own_energy = energies_ref[pl.ds(d // 8, 1), :]
-    own_energy = pltpu.roll(own_energy, (128 - d % 8 * 16) % 128, 1)
-    own_energy = jnp.where(lane < 16, own_energy / HALF_WIDTH, 0.0)
+        name = jnp.where(s < live, ids_ref[s].astype(jnp.float32), -1.0)
+        across = jnp.where((lane & 31) == s, name, across)
+        down[s : s + 1, :] = jnp.full((1, 128), jnp.where(s < live, name, -2.0))
+        strength[s : s + 1, :] = jnp.full((1, 128), energies_ref[ids_ref[s]] * (1.0 / HALF_WIDTH))
+    coef_send[0, 1:2, :] = across
+    coef_send[1, 1:2, :] = across
+    living = jnp.where((lane & 31) < live, 1.0, 0.0)
 
     def halo_copy(h, o, k):
         if k < 4:
@@ -222,13 +233,13 @@
         for k in range(6):
             halo_copy(h, o, k).start()
 
-    def coef_copy(batch, turn, k):
+    def coef_copy(h, j):
         return pltpu.make_async_remote_copy(
-            src_ref=coef_send.at[batch, turn],
-            dst_ref=coef_recv.at[batch, turn, k ^ 1],
-            send_sem=coef_send_sem.at[batch, turn, k],
-            recv_sem=coef_recv_sem.at[batch, turn, k ^ 1],
-            device_id=(near[k], b),
+            src_ref=coef_send.at[h],
+            dst_ref=coef_recv.at[h, j],
+            send_sem=coef_send_sem.at[h, j],
+            recv_sem=coef_recv_sem.at[h, j],
+            device_id=(flip(d, AROUND[j]), b),
             device_id_type=MESH,
         )
 
@@ -250,47 +261,44 @@
         edge_send[h, o, 0] = edges[0:16].astype(jnp.bfloat16)
         edge_send[h, o, 1] = edges[16:32].astype(jnp.bfloat16)
 
-    def project(batch, h, orbs):
+    def project(h):
         def body(x, sums):
             sums = list(sums)
             for y in range(16):
                 row = x * 16 + y
                 columns = proj[:, pl.ds(pl.multiple_of(row * 128, 128), 128)]
-                for i, o in enumerate(orbs):
-                    sums[i] = sums[i] + columns * field[h, o, pl.ds(LOW + row, 1), :]
+                for o in range(ORBS):
+                    sums[o] = sums[o] + columns * field[h, o, pl.ds(LOW + row, 1), :]
             return tuple(sums)
 
         zero = jnp.zeros((SLOTS, 128), jnp.float32)
-        sums = lax.fori_loop(0, 16, body, (zero,) * len(orbs))
-        chosen = selector[...]
-        if len(orbs) < ORBS:
-            coef_send[batch, 0] = jnp.zeros((ORBS, 128), jnp.float32)
-        for i, o in enumerate(orbs):
-            partial = jnp.sum(sums[i], axis=1, keepdims=True)
-            coef_send[batch, 0, o : o + 1, :] = jnp.sum(partial * chosen, axis=0, keepdims=True)
-
-    def send_coefficients(batch, turn):
-        for k in range(6):
-            coef_copy(batch, turn, k).start()
-
-    def own_coefficients(batch):
-        for k in range(6):
-            coef_copy(batch, 0, k).wait_recv()
-        total = pltpu.roll(coef_send[batch, 0], 32, 1)
-        for k in range(6):
-            total = total + pltpu.roll(coef_recv[batch, 0, k], (128 - 16 * (k ^ 1)) % 128, 1)
-        coef_send[batch, 1] = total * own_energy
-        send_coefficients(batch, 1)
-
-    def weigh(batch, orbs):
-        for k in range(6):
-            coef_copy(batch, 1, k).wait_recv()
-        known = pltpu.roll(coef_send[batch, 1], 96, 1)
-        for k in range(6):
-            known = known + pltpu.roll(coef_recv[batch, 1, k], 16 * k, 1)
-        chosen = selector[...]
-        for o in orbs:
-            weight = jnp.sum(chosen * known[o : o + 1, :], axis=1, keepdims=True)
+        sums = lax.fori_loop(0, 16, body, (zero,) * ORBS)
+        slot = lax.broadcasted_iota(jnp.int32, (SLOTS, 128), 0)
+        place = lax.broadcasted_iota(jnp.int32, (SLOTS, 128), 1)
+        laid = zero
+        for o in range(ORBS):
+            partial = jnp.sum(sums[o], axis=1, keepdims=True)
+            laid = jnp.where(place == slot + SLOTS * o, partial, laid)
+        coef_send[h, 0:1, :] = jnp.sum(laid, axis=0, keepdims=True) * living
+
+    def send_coefficients(h):
+        for j in range(len(AROUND)):
+            coef_copy(h, j).start()
+
+    def weigh(h):
+        for j in range(len(AROUND)):
+            coef_copy(h, j).wait_recv()
+        names = down[...]
+        found = jnp.where(names == coef_send[h, 1:2, :], coef_send[h, 0:1, :], 0.0)
+        for j in range(len(AROUND)):
+            found = found + jnp.where(
+                names == coef_recv[h, j, 1:2, :], coef_recv[h, j, 0:1, :], 0.0
+            )
+        found = found * strength[...]
+        place = lax.broadcasted_iota(jnp.int32, (SLOTS, 128), 1)
+        for o in range(ORBS):
+            mine = jnp.where((place >> 5) == o, found, 0.0)
+            weight = jnp.sum(mine, axis=1, keepdims=True)
             splat[o * SLOTS : (o + 1) * SLOTS, :] = jnp.broadcast_to(weight, (SLOTS, 128))
 
     def receive(h, o):
@@ -413,10 +421,12 @@
         loads[o].wait()
     each(0, ORBS, lambda o: prepare(0, o))
     loads[ORBS].wait()
-    project(0, 0, (0, 1, 2, 3))
-    pl.semaphore_wait(barrier, 14 + BANDS - 1)
-    send_coefficients(0, 0)
+    project(0)
+    pl.semaphore_wait(barrier, 14 + len(OTHERS) + BANDS - 1)
+    send_coefficients(0)
     send_halo(0, 0)
+    send_halo(0, 1)
+
     def turn(row, carry):
         proj_rows[pl.ds(row, SLOTS, stride=CELLROWS), :] = proj[
             :, pl.ds(pl.multiple_of(row * 128, 128), 128)
@@ -428,11 +438,9 @@
     diag[...] = (diag[...] + (-0.5 / (SPACING * SPACING) * 3.0 * STENCIL[0] - CENTER)) * (
         1.0 / HALF_WIDTH
     )
-    own_coefficients(0)
-    send_halo(0, 1)
     receive(0, 0)
     send_halo(0, 2)
-    weigh(0, (0, 1, 2, 3))
+    weigh(0)
 
     def first_step(o):
         apply(0, o)
@@ -442,21 +450,20 @@
     receive(0, 1)
     send_halo(0, 3)
     first_step(1)
+    send_halo(1, 0)
     receive(0, 2)
-    send_halo(1, 0)
     first_step(2)
+    send_halo(1, 1)
     receive(0, 3)
     first_step(3)
-    project(1, 1, (0, 1, 2, 3))
-    send_coefficients(1, 0)
-    send_halo(1, 1)
+    project(1)
+    send_coefficients(1)
+    send_halo(1, 2)
 
     receive(1, 0)
-    send_halo(1, 2)
-    own_coefficients(1)
+    send_halo(1, 3)
     receive(1, 1)
-    send_halo(1, 3)
-    weigh(1, (0, 1, 2, 3))
+    weigh(1)
     apply(1, 0)
     apply(1, 1)
     publish(0)
@@ -505,10 +512,9 @@
         total = total + group_high[j]
     margin_ref[...] = total[:, 0:64] * (1.0 / NCELLS)
 
-    for batch in range(2):
-        for turn_ in range(2):
-            for k in range(6):
-                coef_copy(batch, turn_, k).wait_send()
+    for h in range(2):
+        for j in range(len(AROUND)):
+            coef_copy(h, j).wait_send()
 
     def sent(i):
         for k in range(6):
@@ -539,10 +545,9 @@
             jax.ShapeDtypeStruct((ORBS * CELLROWS, 128), jnp.float32),
             jax.ShapeDtypeStruct((ORBS, 64), jnp.float32),
         ),
-        in_specs=[smem, smem] + [hbm] * 4,
+        in_specs=[smem, smem, smem] + [hbm] * 3,
         out_specs=(hbm, vmem),
         scratch_shapes=[
-            pltpu.VMEM((8, 128), jnp.float32),
             pltpu.VMEM((2, ORBS, PADROWS, 128), jnp.float32),
             pltpu.VMEM((ORBS, PADROWS, 128), jnp.float32),
             pltpu.VMEM((SLOTS, 32768), jnp.float32),
@@ -552,11 +557,12 @@
             pltpu.VMEM((2, ORBS, 4, LOW, 128), jnp.bfloat16),
             pltpu.VMEM((2, ORBS, 2, 16, 128), jnp.bfloat16),
             pltpu.VMEM((2, ORBS, 2, 16, 128), jnp.bfloat16),
-            pltpu.VMEM((2, 2, ORBS, 128), jnp.float32),
-            pltpu.VMEM((2, 2, 6, ORBS, 128), jnp.float32),
+            pltpu.VMEM((2, 2, 128), jnp.float32),
+            pltpu.VMEM((2, len(AROUND), 2, 128), jnp.float32),
             pltpu.VMEM((256, 256), jnp.bfloat16),
             pltpu.VMEM((32, 512), jnp.bfloat16),
             pltpu.VMEM((32, 256), jnp.bfloat16),
+            pltpu.VMEM((SLOTS, 128), jnp.float32),
             pltpu.VMEM((SLOTS, 128), jnp.float32),
             pltpu.VMEM((ORBS * SLOTS, 128), jnp.float32),
             pltpu.VMEM((CELLROWS, 128), jnp.float32),
@@ -569,12 +575,12 @@
             pltpu.VMEM((BANDS, ORBS, 128), jnp.float32),
             pltpu.VMEM((8, ORBS, 128), jnp.float32),
             pltpu.VMEM((8, ORBS, 128), jnp.float32),
-            dma((ORBS + 3,)),
+            dma((ORBS + 2,)),
             dma((3,)),
             dma((2, ORBS, 6)),
             dma((2, ORBS, 6)),
-            dma((2, 2, 6)),
-            dma((2, 2, 6)),
+            dma((2, len(AROUND))),
+            dma((2, len(AROUND))),
             dma((3, BANDS)),
             dma((3, BANDS)),
             dma((BANDS,)),
@@ -591,7 +597,7 @@
     )(
         slot_ids,
         slot_count,
-        energies.reshape(8, 128),
+        energies,
         orbitals.reshape(ORBS * CELLROWS, 128),
         potential.reshape(CELLROWS, 128),
         projectors,

time: 102 us -> 98.3 us (0.964)
  Pallas kernels: 101 us -> 96.8 us
    pallas_call x1, Pallas kernels: 99 us -> 94.9 us  [on_device(): pl.pallas_call(kernel, out_shape=(jax.ShapeDtypeStruct((ORBS * CELLROWS,...]
where the time goes in v3:
time: 98.3 us; the launch traced here: 98.1 us
  Pallas kernels  96.8 us (98%)
  between operations  1.29 us (1%)
    pallas_call x1, Pallas kernels, on_device(): pl.pallas_call(kernel, out_shape=(jax.ShapeDtypeStruct((ORBS * CELLROWS,...  94.9 us

profile of v3, /device:TPU:1, one launch (start us, length us, event | category | flops | bytes accessed | tf_op | source)
XLA Modules:
  0.0 98.1 jit_solution(8827166946071849086)
XLA Ops:
  1.3 94.9 %chebyshev.1 = (f32[1024,128]{1,0:T(8,128)}, f32[4,64]{1,0:T(4,128)}) custom-call(s32[32]{0:T(128)} %ids_ref.1, s32[1]{0:T(128)S(6)} %copy.8.count_ref, f32[1024]{0:T(1024)} %energies_ref.1, f32[1024,128]{1,0:T(8,128)} %bitcast.3, f32[256,128]{1,0:T(8,128)} %bitcast.4, f32[32,32768]{1,0:T(8,128)} %proj_ref.1), custom_call_target="tpu_custom_call" | custom-call | tf_op jit(solution)/shard_map/chebyshev/pallas_call | solution.py:542
  96.2 1.9 %results.1 = (f32[1024,128]{1,0:T(8,128)}, f32[4,64]{1,0:T(4,128)}) custom-call(f32[1024,128]{1,0:T(8,128)} %get-tuple-element.6.filt_in, f32[4,64]{1,0:T(4,128)} %get-tuple-element.7.margin_in), custom_call_target="tpu_custom_call" | custom-call | tf_op jit(solution)/shard_map/results/pallas_call | solution.py:605
